TPU v7x, 32 devices: a whole 2x2x4 slice. The times are simulated.
32 devices in a mesh: dp: 2 (over x), expert: 16 (over z, y, core).
Axes of the slice: x: 2, y: 2, z: 4, core: 2. Of those that a mesh axis runs over, the one named last changes fastest.
Arguments:
- out_grads: bfloat16 [4096, 3584], P(('dp', 'expert')), may hold values from -6 to 6
- route_probs: float32 [4096, 4], P(('dp', 'expert')), may hold values from 0.05 to 1
- expert_ids: int32 [4096, 4], P(('dp', 'expert')), may hold values from 0 to 15, all different within a row; in each aligned block of 128 rows (0 to 127, 128 to 255, ...) at most 48 rows name the same one
- saved_inputs: bfloat16 [4096, 4, 1024], P(('dp', 'expert')), may hold values from -0.59765625 to 0.59765625
- w_latent: bfloat16 [16, 3584, 1024], P('expert'), as said below
- block_exponents: int32 [16, 3584, 8], P('expert'), may hold values from -9 to -6, as said below
Outputs:
- input_grads: bfloat16 [4096, 4, 1024], P(('dp', 'expert'))
- weight_grads: float32 [16, 3584, 1024], P('expert', 'dp')
Inputs may be any that keep to these rules, and one draw needn't show every extreme that they name: `expert_ids`: each token names 4 different experts; the 128 tokens of one device name one expert in at most 48 slots, and some expert reaches 48. `block_exponents`: one exponent per 128 consecutive inputs of one output feature. w_latent * 2^(-exponent) lies within 0.45 of a whole number from -9 to 8.
All inputs are finite; a program needn't handle non-finite values.
Results may differ from a plain program's by a relative error of at most 0.012.
Values may be sent and summed in bfloat16 or wider, within the bound.
A program may use at most 128 MiB of HBM per device.

v0:
```python
import jax
import jax.numpy as jnp
from jax import lax
from jax.sharding import PartitionSpec as P

BLK = 128


def dequantize(weight_one, exponent_one):
    shifts = jnp.repeat(-exponent_one, BLK, axis=1)
    powers = jnp.left_shift(jnp.ones_like(shifts), shifts).astype(jnp.float32)
    codes = weight_one.astype(jnp.float32) * powers
    levels = jnp.clip(jnp.floor(codes + 0.5), -8.0, 7.0)
    quantized = (levels / powers).astype(jnp.bfloat16)
    inside = ((codes >= -8.5) & (codes <= 7.5)).astype(jnp.float32)
    return (quantized, inside)


def local(out_grads, route_probs, expert_ids, saved_inputs, w_latent, block_exponents):
    peer_count = lax.axis_size("expert")
    tok_rows, top_count = expert_ids.shape
    feat_width = out_grads.shape[1]
    hidden = saved_inputs.shape[2]
    capacity = tok_rows * top_count * 3 // (2 * peer_count)
    slot_count = tok_rows * top_count
    row_count = peer_count * capacity
    flat_ids = expert_ids.reshape(slot_count)
    onehot = (flat_ids[:, None] == jnp.arange(peer_count, dtype=jnp.int32)[None, :]).astype(
        jnp.int32
    )
    before = jnp.cumsum(onehot, axis=0) - onehot
    position = jnp.sum(before * onehot, axis=1)
    target = flat_ids * capacity + position
    grads = (route_probs[:, :, None] * out_grads[:, None, :].astype(jnp.float32)).astype(
        jnp.bfloat16
    )
    send_grads = (
        jnp.zeros((row_count, feat_width), jnp.bfloat16)
        .at[target]
        .set(grads.reshape(slot_count, feat_width))
    )
    send_inputs = (
        jnp.zeros((row_count, hidden), jnp.bfloat16)
        .at[target]
        .set(saved_inputs.reshape(slot_count, hidden))
    )
    send_grads = send_grads.reshape(peer_count, capacity, feat_width)
    send_inputs = send_inputs.reshape(peer_count, capacity, hidden)
    quantized, inside = dequantize(w_latent[0], block_exponents[0])
    got_grads, got_inputs = (
        lax.all_to_all(send_grads, "expert", split_axis=0, concat_axis=0, tiled=True),
        lax.all_to_all(send_inputs, "expert", split_axis=0, concat_axis=0, tiled=True),
    )
    flat_grads = got_grads.reshape(row_count, feat_width)
    flat_inputs = got_inputs.reshape(row_count, hidden)
    back_rows = jnp.dot(flat_grads, quantized, preferred_element_type=jnp.float32).astype(
        jnp.bfloat16
    )
    returned = lax.all_to_all(
        back_rows.reshape(peer_count, capacity, hidden),
        "expert",
        split_axis=0,
        concat_axis=0,
        tiled=True,
    )
    input_grads = returned.reshape(row_count, hidden)[target].reshape(tok_rows, top_count, hidden)
    replica_count = lax.axis_size("dp")
    share_rows = feat_width // replica_count
    summed = lax.psum_scatter(
        lax.dot_general(
            flat_grads, flat_inputs, (((0,), (0,)), ((), ())), preferred_element_type=jnp.float32
        ).astype(jnp.bfloat16),
        "dp",
        scatter_dimension=0,
        tiled=True,
    ).astype(jnp.float32)
    replica_at = lax.axis_index("dp")
    keep_rows = lax.dynamic_slice_in_dim(inside, replica_at * share_rows, share_rows, 0)
    weight_grads = (summed * keep_rows)[None]
    return (input_grads, weight_grads)


def solution(mesh):
    placed = (
        P(("dp", "expert"), None),
        P(("dp", "expert"), None),
        P(("dp", "expert"), None),
        P(("dp", "expert"), None, None),
        P("expert", None, None),
        P("expert", None, None),
    )
    return jax.shard_map(
        local,
        mesh=mesh,
        in_specs=placed,
        out_specs=(P(("dp", "expert"), None, None), P("expert", "dp", None)),
        check_vma=False,
    )
```

profile of v0, /device:TPU:0, one launch (start us, length us, event | category | flops | bytes accessed | tf_op | source)
XLA Modules:
  0.0 303.7 jit_solution(1245387420249975323)
XLA Ops:
  7.9 0.8 copy.10
  9.2 1.2 reduce-window.6
  10.6 1.3 reshape.138
  12.0 3.9 %scatter_custom_fusion.1 = bf16[768,1024]{1,0:T(8,128)(2,1)} fusion(s32[512]{0:T(512)S(1)} %bitcast.51, bf16[512,1024]{1,0:T(8,128)(2,1)S(1)} %reshape.138, bf16[]{:T(256)} %constant.14.clone.1), kind=kCustom, calls=%fused_computation.21 | custom fusion | bytes 1572866 | tf_op jit(solution)/shard_map/scatter | solution.py:45
  16.0 7.4 %all-to-all-start.2 = ((bf16[16,48,1024]{2,1,0:T(8,128)(2,1)}), bf16[16,48,1024]{2,1,0:T(8,128)(2,1)S(1)}, u32[]{:S(2)}, u32[]{:S(2)}) async-start(bf16[16,48,1024]{2,1,0:T(8,128)(2,1)} %bitcast.9), calls=%async_computation.2 | async-start | bytes 3145728 | tf_op jit(solution)/shard_map/all_to_all | solution.py:52
  23.4 4.0 %mul.55 = f32[128,4,3584]{2,1,0:T(4,128)} broadcast(bf16[128,3584]{1,0:T(8,128)(2,1)S(1)} %copy-done.1), dimensions={0,2} | broadcast | bytes 8257536 | tf_op jit(solution)/shard_map/mul | solution.py:34
  27.4 9.0 %mul.56 = f32[512,3584]{1,0:T(8,128)} reshape(f32[128,4,3584]{2,1,0:T(4,128)} %mul.55) | data formatting | bytes 14680064 | tf_op jit(solution)/shard_map/mul | solution.py:34
  36.7 11.4 %scatter_custom_fusion = bf16[768,3584]{1,0:T(8,128)(2,1)} fusion(s32[512]{0:T(512)S(1)} %bitcast.52, f32[512,3584]{1,0:T(8,128)} %mul.56, f32[512]{0:T(512)S(1)} %mul.53, bf16[]{:T(256)} %constant.14.clone.1), kind=kCustom, calls=%fused_computation.17 | custom fusion | flops 3670016 | bytes 12847106 | tf_op jit(solution)/shard_map/scatter | solution.py:40
  48.0 7.3 %all-to-all-done.2 = bf16[16,48,1024]{2,1,0:T(8,128)(2,1)S(1)} async-done(((bf16[16,48,1024]{2,1,0:T(8,128)(2,1)}), bf16[16,48,1024]{2,1,0:T(8,128)(2,1)S(1)}, u32[]{:S(2)}, u32[]{:S(2)}) %all-to-all-start.2) | async-done | bytes 1572896 | tf_op jit(solution)/shard_map/all_to_all | solution.py:52
  55.3 130.5 %all_to_all.15 = bf16[16,48,3584]{2,1,0:T(8,128)(2,1)S(1)} all-to-all(bf16[16,48,3584]{2,1,0:T(8,128)(2,1)} %bitcast.49), channel_id=1, replica_groups=mesh['dp'=2,'expert'=16] {'expert'}, dimensions={0} | all-to-all | bytes 11010048 | tf_op jit(solution)/shard_map/all_to_all | solution.py:51
  185.9 2.4 copy-done
  188.2 8.0 %bitcast_convert_fusion = bf16[3584,1024]{1,0:T(8,128)(2,1)} fusion(bf16[16,48,3584]{2,1,0:T(8,128)(2,1)S(1)} %all_to_all.15, bf16[16,48,1024]{2,1,0:T(8,128)(2,1)S(1)} %all-to-all-done.2), kind=kOutput, calls=%fused_computation.10 | convolution fusion | flops 5640814592 | bytes 14417920 | tf_op jit(solution)/shard_map/dot_general | solution.py:70
  196.3 0.9 copy-done.2
  197.7 9.4 %broadcast_in_dim.23 = f32[3584,8,128]{2,1,0:T(8,128)} broadcast(f32[3584,8]{1,0:T(8,128)S(1)} %copy.14), dimensions={0,1} | broadcast | bytes 14794752 | tf_op jit(solution)/shard_map/broadcast_in_dim | solution.py:10
  207.1 15.9 %convert_element_type.71 = f32[1,3584,1024]{2,1,0:T(8,128)} reshape(f32[3584,8,128]{2,1,0:T(8,128)} %broadcast_in_dim.23) | data formatting | bytes 29360128 | tf_op jit(solution)/shard_map/convert_element_type | solution.py:11
  223.0 13.3 %fusion.11 = bf16[768,1024]{1,0:T(8,128)(2,1)} fusion(bf16[768,3584]{1,0:T(8,128)(2,1)} %bitcast.50, f32[1,3584,1024]{2,1,0:T(8,128)} %convert_element_type.71, bf16[1,3584,1024]{2,1,0:T(8,128)(2,1)} %param.10), kind=kOutput, calls=%fused_computation.20 | convolution fusion | flops 5663621120 | bytes 29097984 | tf_op jit(solution)/shard_map/dot_general | solution.py:56
  236.4 4.3 %all-to-all-start.1 = ((bf16[16,48,1024]{2,1,0:T(8,128)(2,1)}), bf16[16,48,1024]{2,1,0:T(8,128)(2,1)S(1)}, u32[]{:S(2)}, u32[]{:S(2)}) async-start(bf16[16,48,1024]{2,1,0:T(8,128)(2,1)} %bitcast.7), calls=%async_computation.1 | async-start | bytes 3145728 | tf_op jit(solution)/shard_map/all_to_all | solution.py:59
  240.7 14.4 %copy.19 = f32[448,8,8,128]{3,1,2,0:T(8,128)} copy(f32[448,8,8,128]{3,2,1,0:T(8,128)} %bitcast.46) | data formatting | bytes 29360128
  255.1 10.2 %convert_bitcast_fusion = f32[3584,1024]{1,0:T(8,128)} fusion(bf16[1,3584,1024]{2,1,0:T(8,128)(2,1)} %param.10), kind=kLoop, calls=%fused_computation.3 | loop fusion | flops 3670016 | bytes 22020096 | tf_op jit(solution)/shard_map/convert_element_type | solution.py:12
  265.3 7.4 %all-to-all-done.1 = bf16[16,48,1024]{2,1,0:T(8,128)(2,1)S(1)} async-done(((bf16[16,48,1024]{2,1,0:T(8,128)(2,1)}), bf16[16,48,1024]{2,1,0:T(8,128)(2,1)S(1)}, u32[]{:S(2)}, u32[]{:S(2)}) %all-to-all-start.1) | async-done | bytes 1572896 | tf_op jit(solution)/shard_map/all_to_all | solution.py:59
  272.7 2.0 gather_fusion
  274.7 1.2 reshape.114
  276.0 8.6 %reduce-scatter.2.cloned.1.call-done = bf16[1792,1024]{1,0:T(8,128)(2,1)} async-done(((bf16[3584,1024]{1,0:T(8,128)(2,1)}), bf16[1792,1024]{1,0:T(8,128)(2,1)}) %reduce-scatter.2.cloned.1.call-update) | async-done | bytes 3670032 | tf_op jit(solution)/shard_map/reduce_scatter | solution.py:69
  284.5 12.3 %multiply_bitcast_fusion = f32[1,1792,1024]{2,1,0:T(8,128)} fusion(bf16[1792,1024]{1,0:T(8,128)(2,1)} %reduce-scatter.2.cloned.1.call-done, f32[3584,1024]{1,0:T(8,128)} %bitcast.48, s32[]{:T(128)S(6)} %select_n.16, f32[3584,1024]{1,0:T(8,128)} %convert_bitcast_fusion), kind=kLoop, calls=%fused_computation.15 | loop fusion | flops 12845056 | bytes 25690116 | tf_op jit(solution)/shard_map/broadcast_in_dim | solution.py:79
  (24 shorter events, 2.4 us)
Async XLA Ops:
  7.2 16.3 %copy-start.1 = (bf16[128,3584]{1,0:T(8,128)(2,1)S(1)}, bf16[128,3584]{1,0:T(8,128)(2,1)}, u32[]{:S(2)}) copy-start(bf16[128,3584]{1,0:T(8,128)(2,1)} %param.6) | copy-start | bytes 2752516
  16.0 39.4 %all-to-all-start.2 = ((bf16[16,48,1024]{2,1,0:T(8,128)(2,1)}), bf16[16,48,1024]{2,1,0:T(8,128)(2,1)S(1)}, u32[]{:S(2)}, u32[]{:S(2)}) async-start(bf16[16,48,1024]{2,1,0:T(8,128)(2,1)} %bitcast.9), calls=%async_computation.2 | async-start | bytes 3145728 | tf_op jit(solution)/shard_map/all_to_all | solution.py:52
  23.4 261.2 %reduce-scatter.2.cloned.1.call-start = ((), (), s32[]{:S(2)}) async-start(), calls=%async_computation.4 | async-start | bytes 11010048 | tf_op jit(solution)/shard_map/reduce_scatter | solution.py:69
  27.4 9.0 %copy-start.3 = (f32[128,4]{0,1:T(4,128)S(1)}, f32[128,4]{0,1:T(4,128)}, u32[]{:S(2)}) copy-start(f32[128,4]{0,1:T(4,128)} %param.7) | copy-start | bytes 6148
  185.8 2.4 copy-start
  196.3 0.9 copy-start.2
  236.4 36.3 %all-to-all-start.1 = ((bf16[16,48,1024]{2,1,0:T(8,128)(2,1)}), bf16[16,48,1024]{2,1,0:T(8,128)(2,1)S(1)}, u32[]{:S(2)}, u32[]{:S(2)}) async-start(bf16[16,48,1024]{2,1,0:T(8,128)(2,1)} %bitcast.7), calls=%async_computation.1 | async-start | bytes 3145728 | tf_op jit(solution)/shard_map/all_to_all | solution.py:59
Sparse Core Ops, SparseCore 0:
  196.4 88.0 reduce-scatter.1
where the time goes:
time: 305 us; the launch traced here: 304 us
  blocking collectives  131 us (43%)
  local copies, waits for them, and re-layouts  66.7 us (22%)
  other arithmetic  35.9 us (12%)
  waiting for transfers between devices  23.3 us (8%)
  matrix products  21.4 us (7%)
  between operations  14.1 us (5%)
  starting transfers between devices  11.8 us (4%)
    all_to_all x1, blocking collectives, local(): lax.all_to_all(send_grads, 'expert', split_axis=0, concat_axis=0, tiled=T...  131 us
    unnamed x11, local copies, waits for them, and re-layouts  18.6 us
    convert_element_type x2, local copies, waits for them, and re-layouts, dequantize(): powers = jnp.left_shift(jnp.ones_like(shifts), shifts).astype(jnp.float32)  16.4 us
    dot_general x1, matrix products, local(): jnp.dot(flat_grads, quantized, preferred_element_type=jnp.float32)  13.3 us
    mul x3, local copies, waits for them, and re-layouts, local(): route_probs[:, :, None] * out_grads[:, None, :].astype(jnp.float32)  13.1 us
    broadcast_in_dim x1, other arithmetic, local(): weight_grads = (summed * keep_rows)[None]  12.3 us
    scatter x1, other arithmetic, local(): send_grads = jnp.zeros((row_count, feat_width), jnp.bfloat16).at[target]....  11.4 us
    convert_element_type x1, other arithmetic, dequantize(): codes = weight_one.astype(jnp.float32) * powers  10.2 us
  transfers between devices with their start and end apart: 3, of which 3 were waited for; matrix products, arithmetic and copies ran while one was open for 30% of the time, Pallas kernels for 0%

commit v1 on v0

v1 whole, which is shorter than its diff:
```python
import functools

import jax
import jax.numpy as jnp
from jax import lax
from jax.experimental import pallas as pl
from jax.experimental.pallas import tpu as pltpu
from jax.sharding import PartitionSpec as P

BLK = 128
PLANE = 4
PIECES = 2
VMEM_LIMIT = 56 * 1024 * 1024


def pack_kernel(n, capp, ids_ref, probs_ref, saved_ref, send_ref, meta_ref):
    slots = ids_ref.shape[1]
    ids = ids_ref[...]
    expert_rows = lax.broadcasted_iota(jnp.int32, (n, slots), 0)
    onehot = (expert_rows == ids).astype(jnp.float32)
    earlier = lax.broadcasted_iota(jnp.int32, (slots, slots), 0)
    later = lax.broadcasted_iota(jnp.int32, (slots, slots), 1)
    before = jnp.dot(
        onehot.astype(jnp.bfloat16),
        (earlier < later).astype(jnp.float32).astype(jnp.bfloat16),
        preferred_element_type=jnp.float32,
    )
    position = jnp.sum(before * onehot, axis=0, keepdims=True)
    target = ids.astype(jnp.float32) * float(capp) + position
    meta_ref[...] = jnp.zeros_like(meta_ref)
    meta_ref[0:1, :] = target
    meta_ref[1:2, :] = probs_ref[...]
    target = target.astype(jnp.int32)
    places = lax.broadcasted_iota(jnp.int32, (capp, slots), 0)

    @pl.loop(0, n)
    def _(e):
        pick = (places + e * capp == target).astype(jnp.float32).astype(jnp.bfloat16)
        send_ref[e] = jnp.dot(pick, saved_ref[...], preferred_element_type=jnp.float32).astype(
            jnp.bfloat16
        )


def exchange_kernel(
    n, own, xs, meta, g, x, m, local_sem, up_sem, down_sem, y_sem, core_sem, x_send, x_recv, m_send, m_recv, g_recv
):
    me = lax.axis_index("expert")
    depth = n // PLANE
    z = me // PLANE
    lane = lax.rem(me, PLANE)
    core_lane = lane + 1 - 2 * lax.rem(lane, 2)
    y_lane = lax.rem(lane + 2, PLANE)
    core_mate = z * PLANE + core_lane
    y_mate = z * PLANE + y_lane
    rows = own.shape[0] // PIECES

    barrier = pltpu.get_barrier_semaphore()
    for d in range(1, n):
        pl.semaphore_signal(barrier, inc=1, device_id={"expert": lax.rem(me + d, n)})
    pl.semaphore_wait(barrier, n - 1)

    def cp(block, k, dest, send, from_own=False):
        part = pl.ds(k * rows, rows)
        return pltpu.make_async_remote_copy(
            src_ref=own.at[part] if from_own else g.at[block, part],
            dst_ref=g.at[block, part],
            send_sem=send,
            recv_sem=g_recv.at[block, k],
            device_id={"expert": dest},
        )

    def got(block, k):
        cp(block, k, me, up_sem.at[0, k]).wait_recv()

    def hand_on(bz, k, up, down, from_own=False):
        block = bz * PLANE + lane
        if up:
            @pl.when(z + 1 < depth)
            def _():
                cp(block, k, me + PLANE, up_sem.at[bz, k], from_own).start()
        if down:
            @pl.when(z >= 1)
            def _():
                cp(block, k, me - PLANE, down_sem.at[bz, k], from_own).start()
        cp(block, k, y_mate, y_sem.at[bz, k], from_own).start()
        cp(block, k, core_mate, core_sem.at[bz, k], from_own).start()

    for k in range(PIECES):
        hand_on(z, k, True, True, from_own=True)

    locals_ = [
        pltpu.make_async_copy(own, g.at[me], local_sem.at[0]),
        pltpu.make_async_copy(xs.at[me], x.at[me], local_sem.at[1]),
        pltpu.make_async_copy(meta, m.at[me], local_sem.at[2]),
    ]
    for c in locals_:
        c.start()

    def xcp(d):
        dest = lax.rem(me + d, n)
        return pltpu.make_async_remote_copy(
            src_ref=xs.at[dest], dst_ref=x.at[me], send_sem=x_send.at[d], recv_sem=x_recv.at[me],
            device_id={"expert": dest},
        )

    def mcp(d):
        return pltpu.make_async_remote_copy(
            src_ref=meta, dst_ref=m.at[me], send_sem=m_send.at[d], recv_sem=m_recv.at[me],
            device_id={"expert": lax.rem(me + d, n)},
        )

    for d in range(1, n):
        mcp(d).start()
        xcp(d).start()

    def relay(bz, k):
        block = bz * PLANE + y_lane
        got(block, k)
        cp(block, k, core_mate, core_sem.at[depth + bz, k]).start()

    for step in range(1, depth + 1):
        for k in range(PIECES):
            if step < depth:
                @pl.when(z - step >= 0)
                def _():
                    got((z - step) * PLANE + lane, k)
                    hand_on(z - step, k, True, False)

                @pl.when(z + step < depth)
                def _():
                    got((z + step) * PLANE + lane, k)
                    hand_on(z + step, k, False, True)
            last = step - 1
            @pl.when(z - last >= 0)
            def _():
                relay(z - last, k)

            if last:
                @pl.when(z + last < depth)
                def _():
                    relay(z + last, k)

    for bz in range(depth):
        for k in range(PIECES):
            got(bz * PLANE + core_lane, k)
            got(bz * PLANE + lax.rem(core_lane + 2, PLANE), k)
    for d in range(1, n):
        peer = lax.rem(me + d, n)
        pltpu.make_async_remote_copy(
            src_ref=xs.at[peer], dst_ref=x.at[peer], send_sem=x_send.at[d], recv_sem=x_recv.at[peer],
            device_id={"expert": peer},
        ).wait_recv()
        pltpu.make_async_remote_copy(
            src_ref=meta, dst_ref=m.at[peer], send_sem=m_send.at[d], recv_sem=m_recv.at[peer],
            device_id={"expert": peer},
        ).wait_recv()
    for d in range(1, n):
        xcp(d).wait_send()
        mcp(d).wait_send()
    for bz in range(depth):
        for k in range(PIECES):
            block = bz * PLANE + lane

            @pl.when((z + 1 < depth) & (bz <= z))
            def _():
                cp(block, k, me, up_sem.at[bz, k]).wait_send()

            @pl.when((z >= 1) & (bz >= z))
            def _():
                cp(block, k, me, down_sem.at[bz, k]).wait_send()

            cp(block, k, y_mate, y_sem.at[bz, k]).wait_send()
            cp(block, k, core_mate, core_sem.at[bz, k]).wait_send()
            cp(block, k, core_mate, core_sem.at[depth + bz, k]).wait_send()
    for c in locals_:
        c.wait()


def powers_of(exponents):
    one = jnp.ones_like(exponents)
    up = jnp.left_shift(one, -exponents).astype(jnp.float32)
    down = jnp.left_shift(one, exponents + 16).astype(jnp.float32) * (2.0**-16)
    return up, down


def expert_kernel(n, capp, top, me_ref, m_ref, g_ref, x_ref, w_ref, e_ref, back_ref, part_ref, sel, prob, sg, wq, acc):
    step = pl.program_id(0)
    tok = g_ref.shape[0] // n
    slots = m_ref.shape[2]

    @pl.when(step == 0)
    def _():
        acc[...] = jnp.zeros_like(acc)
        places = lax.broadcasted_iota(jnp.int32, (capp, slots), 0) + me_ref[0] * capp
        token_of = lax.broadcasted_iota(jnp.int32, (slots, tok), 0)
        first = lax.broadcasted_iota(jnp.int32, (slots, tok), 1) * top
        owner = ((token_of >= first) & (token_of < first + top)).astype(jnp.float32).astype(jnp.bfloat16)

        @pl.loop(0, n)
        def _(s):
            here = (places == m_ref[s, 0:1, :].astype(jnp.int32)).astype(jnp.float32)
            sel[s] = jnp.dot(
                here.astype(jnp.bfloat16), owner, preferred_element_type=jnp.float32
            ).astype(jnp.bfloat16)
            weight = jnp.sum(here * m_ref[s, 1:2, :], axis=1, keepdims=True)
            prob[s] = jnp.broadcast_to(weight, prob.shape[1:])

    for s in range(n):
        picked = jnp.dot(sel[s], g_ref[s * tok : (s + 1) * tok, :], preferred_element_type=jnp.float32)
        sg[s * capp : (s + 1) * capp, :] = (picked * prob[s][:, 0:1]).astype(jnp.bfloat16)
    up, down = powers_of(e_ref[...])
    for j in range(e_ref.shape[1]):
        cols = slice(j * BLK, (j + 1) * BLK)
        codes = w_ref[:, cols].astype(jnp.float32) * up[:, j : j + 1]
        levels = jnp.clip(jnp.floor(codes + 0.5), -8.0, 7.0)
        wq[:, cols] = (levels * down[:, j : j + 1]).astype(jnp.bfloat16)
    acc[...] += jnp.dot(sg[...], wq[...], preferred_element_type=jnp.float32)
    part_ref[...] = lax.dot_general(
        sg[...], x_ref[...], (((0,), (0,)), ((), ())), preferred_element_type=jnp.float32
    ).astype(jnp.bfloat16)

    @pl.when(step == pl.num_programs(0) - 1)
    def _():
        back_ref[...] = acc[...].astype(jnp.bfloat16)


def keep_kernel(at_ref, s_ref, w_ref, e_ref, o_ref):
    up, _ = powers_of(e_ref[...])
    for j in range(e_ref.shape[1]):
        cols = slice(j * BLK, (j + 1) * BLK)
        codes = w_ref[:, cols].astype(jnp.float32) * up[:, j : j + 1]
        inside = ((codes >= -8.5) & (codes <= 7.5)).astype(jnp.float32)
        o_ref[:, cols] = s_ref[:, cols].astype(jnp.float32) * inside


def tile_of(size, most):
    return max(t for t in range(16, most + 1, 16) if size % t == 0)


def local(out_grads, route_probs, expert_ids, saved_inputs, w_latent, block_exponents):
    n = lax.axis_size("expert")
    tok, top = expert_ids.shape
    width = out_grads.shape[1]
    hidden = saved_inputs.shape[2]
    slots = tok * top
    capacity = tok * top * 3 // (2 * n)
    capp = -(-capacity // 16) * 16
    blocks = block_exponents.shape[2]
    bf16, f32 = jnp.bfloat16, jnp.float32
    vmem = pl.BlockSpec(memory_space=pltpu.VMEM)
    anyspace = pl.BlockSpec(memory_space=pl.ANY)
    params = functools.partial(pltpu.CompilerParams, vmem_limit_bytes=VMEM_LIMIT)

    sends, meta = pl.pallas_call(
        functools.partial(pack_kernel, n, capp),
        out_shape=(
            jax.ShapeDtypeStruct((n, capp, hidden), bf16),
            jax.ShapeDtypeStruct((8, slots), f32),
        ),
        in_specs=[vmem] * 3,
        out_specs=(vmem, vmem),
        compiler_params=params(),
        name="pack_slots",
    )(expert_ids.reshape(1, slots), route_probs.reshape(1, slots), saved_inputs.reshape(slots, hidden))

    depth = n // PLANE
    dma = pltpu.SemaphoreType.DMA
    g, x, m = pl.pallas_call(
        functools.partial(exchange_kernel, n),
        out_shape=(
            jax.ShapeDtypeStruct((n, tok, width), bf16),
            jax.ShapeDtypeStruct((n, capp, hidden), bf16),
            jax.ShapeDtypeStruct((n, 8, slots), f32),
        ),
        in_specs=[anyspace] * 3,
        out_specs=(anyspace,) * 3,
        scratch_shapes=[
            dma((3,)),
            dma((depth, PIECES)),
            dma((depth, PIECES)),
            dma((depth, PIECES)),
            dma((2 * depth, PIECES)),
            dma((n,)),
            dma((n,)),
            dma((n,)),
            dma((n,)),
            dma((n, PIECES)),
        ],
        compiler_params=pltpu.CompilerParams(collective_id=0, has_side_effects=True),
        name="exchange",
    )(out_grads, sends, meta)

    me = lax.axis_index("expert").astype(jnp.int32).reshape(1)
    chunk = 512
    back, partial = pl.pallas_call(
        functools.partial(expert_kernel, n, capp, top),
        grid=(width // chunk,),
        out_shape=(
            jax.ShapeDtypeStruct((n * capp, hidden), bf16),
            jax.ShapeDtypeStruct((width, hidden), bf16),
        ),
        in_specs=[
            pl.BlockSpec(memory_space=pltpu.SMEM),
            pl.BlockSpec((n, 8, slots), lambda i: (0, 0, 0)),
            pl.BlockSpec((n * tok, chunk), lambda i: (0, i)),
            pl.BlockSpec((n * capp, hidden), lambda i: (0, 0)),
            pl.BlockSpec((chunk, hidden), lambda i: (i, 0)),
            pl.BlockSpec((chunk, blocks), lambda i: (i, 0)),
        ],
        out_specs=(
            pl.BlockSpec((n * capp, hidden), lambda i: (0, 0)),
            pl.BlockSpec((chunk, hidden), lambda i: (i, 0)),
        ),
        scratch_shapes=[
            pltpu.VMEM((n, capp, tok), bf16),
            pltpu.VMEM((n, capp, 128), f32),
            pltpu.VMEM((n * capp, chunk), bf16),
            pltpu.VMEM((chunk, hidden), bf16),
            pltpu.VMEM((n * capp, hidden), f32),
        ],
        compiler_params=params(),
        name="expert",
    )(me, m, g.reshape(n * tok, width), x.reshape(n * capp, hidden), w_latent[0], block_exponents[0])

    returned = lax.all_to_all(
        back.reshape(n, capp, hidden), "expert", split_axis=0, concat_axis=0, tiled=True
    )
    target = meta[0].astype(jnp.int32)
    input_grads = returned.reshape(n * capp, hidden)[target].reshape(tok, top, hidden)

    summed = lax.psum_scatter(partial, "dp", scatter_dimension=0, tiled=True)
    share = summed.shape[0]
    tile = tile_of(share, 256)
    tiles = share // tile
    at = (lax.axis_index("dp") * tiles).astype(jnp.int32).reshape(1)
    weight_grads = pl.pallas_call(
        keep_kernel,
        grid_spec=pltpu.PrefetchScalarGridSpec(
            num_scalar_prefetch=1,
            grid=(tiles,),
            in_specs=[
                pl.BlockSpec((tile, hidden), lambda i, at: (i, 0)),
                pl.BlockSpec((tile, hidden), lambda i, at: (at[0] + i, 0)),
                pl.BlockSpec((tile, blocks), lambda i, at: (at[0] + i, 0)),
            ],
            out_specs=pl.BlockSpec((tile, hidden), lambda i, at: (i, 0)),
        ),
        out_shape=jax.ShapeDtypeStruct((share, hidden), f32),
        compiler_params=params(),
        name="keep",
    )(at, summed, w_latent[0], block_exponents[0])
    return (input_grads, weight_grads[None])


def solution(mesh):
    placed = (
        P(("dp", "expert"), None),
        P(("dp", "expert"), None),
        P(("dp", "expert"), None),
        P(("dp", "expert"), None, None),
        P("expert", None, None),
        P("expert", None, None),
    )
    return jax.shard_map(
        local,
        mesh=mesh,
        in_specs=placed,
        out_specs=(P(("dp", "expert"), None, None), P("expert", "dp", None)),
        check_vma=False,
    )
```

time: 305 us -> 268 us (0.88)
  Pallas kernels: 0 us -> 157 us
  blocking collectives: 131 us -> 0 us
  waiting for transfers between devices: 23.3 us -> 79.9 us
  local copies, waits for them, and re-layouts: 66.7 us -> 10.1 us
  other arithmetic: 35.9 us -> 0.73 us
  matrix products: 21.4 us -> 0 us
  starting transfers between devices: 11.8 us -> 4.88 us
    pallas_call x0 -> x4, Pallas kernels: none -> 157 us  [the longest x1 112 us: local(): pl.pallas_call(functools.partial(exchange_kernel, n), out_shape=(jax.Shap...]
    all_to_all x1 -> x0, blocking collectives: 131 us -> none  [local(): lax.all_to_all(send_grads, 'expert', split_axis=0, concat_axis=0, tiled=T...]
    reduce_scatter x1, waiting for transfers between devices: 8.59 us -> 48.7 us  [local(): summed = lax.psum_scatter(partial, 'dp', scatter_dimension=0, tiled=True)]
    dot_general x2 -> x0, matrix products: 21.4 us -> none  [the longest x1 13.3 us: local(): jnp.dot(flat_grads, quantized, preferred_element_type=jnp.float32)]
    all_to_all x2 -> x1, waiting for transfers between devices: 14.7 us -> 31.2 us  [local(): lax.all_to_all(back.reshape(n, capp, hidden), 'expert', split_axis=0, con...]
    convert_element_type x2 -> x0, local copies, waits for them, and re-layouts: 16.4 us -> none  [dequantize(): powers = jnp.left_shift(jnp.ones_like(shifts), shifts).astype(jnp.float32)]
    unnamed x11 -> x5, local copies, waits for them, and re-layouts: 18.6 us -> 3.35 us
    mul x5 -> x0, local copies, waits for them, and re-layouts: 13.3 us -> none  [the longest x3 13.1 us: local(): route_probs[:, :, None] * out_grads[:, None, :].astype(jnp.float32)]
  transfers between devices with their start and end apart: 3 -> 2, of which waited for: 3 -> 2; matrix products, arithmetic and copies ran while one was open for 30% -> 1% of each run, Pallas kernels for 0% -> 0%
where the time goes in v1:
time: 268 us; the launch traced here: 267 us
  Pallas kernels  157 us (59%)
  waiting for transfers between devices  79.9 us (30%)
  between operations  14.1 us (5%)
  local copies, waits for them, and re-layouts  10.1 us (4%)
  starting transfers between devices  4.88 us (2%)
    pallas_call x1, Pallas kernels, local(): pl.pallas_call(functools.partial(exchange_kernel, n), out_shape=(jax.Shap...  112 us
    reduce_scatter x1, waiting for transfers between devices, local(): summed = lax.psum_scatter(partial, 'dp', scatter_dimension=0, tiled=True)  48.7 us
    all_to_all x1, waiting for transfers between devices, local(): lax.all_to_all(back.reshape(n, capp, hidden), 'expert', split_axis=0, con...  31.2 us
    pallas_call x1, Pallas kernels, local(): pl.pallas_call(functools.partial(expert_kernel, n, capp, top), grid=(widt...  28.9 us
    pallas_call x1, Pallas kernels, local(): pl.pallas_call(keep_kernel, grid_spec=pltpu.PrefetchScalarGridSpec(num_sc...  9.58 us
    pallas_call x1, Pallas kernels, local(): pl.pallas_call(functools.partial(pack_kernel, n, capp), out_shape=(jax.Sh...  7.31 us
  transfers between devices with their start and end apart: 2, of which 2 were waited for; matrix products, arithmetic and copies ran while one was open for 1% of the time, Pallas kernels for 0%

profile of v1, /device:TPU:0, one launch (start us, length us, event | category | flops | bytes accessed | tf_op | source)
XLA Modules:
  0.0 267.1 jit_solution(8624460609751344868)
XLA Ops:
  7.2 0.0 copy-start
  7.2 0.0 reduce-scatter.2.cloned.1.call-start
  7.2 0.8 copy.12
  8.0 0.7 reshape.56.probs_ref
  8.7 0.8 copy.11
  9.5 0.7 reshape.55.ids_ref
  10.2 2.1 reshape.57.saved_ref
  12.3 0.0 copy-done
  12.3 1.8 copy.13
  14.1 7.3 %pack_slots.1 = (bf16[16,48,1024]{2,1,0:T(8,128)(2,1)}, f32[8,512]{1,0:T(8,128)}) custom-call(s32[1,512]{1,0:T(1,128)} %reshape.55.ids_ref, f32[1,512]{1,0:T(1,128)} %reshape.56.probs_ref, bf16[512,1024]{1,0:T(8,128)(2,1)} %reshape.57.saved_ref), custom_call_target="tpu_custom_call" | custom-call | tf_op jit(solution)/shard_map/pack_slots/pallas_call | solution.py:254
  21.4 111.5 %exchange.1 = (bf16[16,128,3584]{2,1,0:T(8,128)(2,1)}, bf16[16,48,1024]{2,1,0:T(8,128)(2,1)}, f32[16,8,512]{2,1,0:T(8,128)}) custom-call(bf16[128,3584]{1,0:T(8,128)(2,1)} %own.1, bf16[16,48,1024]{2,1,0:T(8,128)(2,1)} %get-tuple-element.9.xs, f32[8,512]{1,0:T(8,128)} %get-tuple-element.10.meta), custom_call_target="tpu_custom_call" | custom-call | tf_op jit(solution)/shard_map/exchange/pallas_call | solution.py:268
  132.9 28.9 %expert.1 = (bf16[768,1024]{1,0:T(8,128)(2,1)}, bf16[3584,1024]{1,0:T(8,128)(2,1)}) custom-call(s32[1]{0:T(128)} %bitcast.me_ref, f32[16,8,512]{2,1,0:T(8,128)} %get-tuple-element.11.m_ref, bf16[2048,3584]{1,0:T(8,128)(2,1)} %bitcast.17, bf16[768,1024]{1,0:T(8,128)(2,1)} %bitcast.19, bf16[3584,1024]{1,0:T(8,128)(2,1)} %bitcast.13, s32[3584,8]{1,0:T(8,128)} %bitcast.15), custom_call_target="tpu_custom_call" | custom-call | tf_op jit(solution)/shard_map/expert/pallas_call | solution.py:295
  161.9 0.0 reduce-scatter.2.cloned.1.call-update
  161.9 4.8 %all-to-all-start = ((bf16[16,48,1024]{2,1,0:T(8,128)(2,1)}), bf16[16,48,1024]{2,1,0:T(8,128)(2,1)S(1)}, u32[]{:S(2)}, u32[]{:S(2)}) async-start(bf16[16,48,1024]{2,1,0:T(8,128)(2,1)} %bitcast.5), calls=%async_computation | async-start | bytes 3145728 | tf_op jit(solution)/shard_map/all_to_all | solution.py:325
  166.8 0.7 compare_select_fusion
  167.5 31.2 %all-to-all-done = bf16[16,48,1024]{2,1,0:T(8,128)(2,1)S(1)} async-done(((bf16[16,48,1024]{2,1,0:T(8,128)(2,1)}), bf16[16,48,1024]{2,1,0:T(8,128)(2,1)S(1)}, u32[]{:S(2)}, u32[]{:S(2)}) %all-to-all-start) | async-done | bytes 1572896 | tf_op jit(solution)/shard_map/all_to_all | solution.py:325
  198.7 2.0 gather_fusion
  200.8 1.2 reshape.62
  202.0 48.7 %reduce-scatter.2.cloned.1.call-done.s_ref = bf16[1792,1024]{1,0:T(8,128)(2,1)} async-done(((bf16[3584,1024]{1,0:T(8,128)(2,1)}), bf16[1792,1024]{1,0:T(8,128)(2,1)}) %reduce-scatter.2.cloned.1.call-update) | async-done | bytes 3670032 | tf_op jit(solution)/shard_map/reduce_scatter | solution.py:331
  250.7 9.6 %keep.1 = f32[1792,1024]{1,0:T(8,128)} custom-call(s32[1]{0:T(128)} %bitcast.9.at_ref, bf16[1792,1024]{1,0:T(8,128)(2,1)} %reduce-scatter.2.cloned.1.call-done.s_ref, bf16[3584,1024]{1,0:T(8,128)(2,1)} %bitcast.14, s32[3584,8]{1,0:T(8,128)} %bitcast.16), custom_call_target="tpu_custom_call" | custom-call | tf_op jit(solution)/shard_map/keep/pallas_call | solution.py:336
  (1 shorter events, 0.0 us)
Async XLA Ops:
  7.2 5.2 %copy-start = (s32[1,3584,8]{1,2,0:T(8,128)S(1)}, s32[1,3584,8]{1,2,0:T(8,128)}, u32[]{:S(2)}) copy-start(s32[1,3584,8]{1,2,0:T(8,128)} %param.11) | copy-start | bytes 344068
  7.2 243.5 %reduce-scatter.2.cloned.1.call-start = ((), (), s32[]{:S(2)}) async-start(), calls=%async_computation.2 | async-start | bytes 11010048 | tf_op jit(solution)/shard_map/reduce_scatter | solution.py:331
  161.9 36.8 %all-to-all-start = ((bf16[16,48,1024]{2,1,0:T(8,128)(2,1)}), bf16[16,48,1024]{2,1,0:T(8,128)(2,1)S(1)}, u32[]{:S(2)}, u32[]{:S(2)}) async-start(bf16[16,48,1024]{2,1,0:T(8,128)(2,1)} %bitcast.5), calls=%async_computation | async-start | bytes 3145728 | tf_op jit(solution)/shard_map/all_to_all | solution.py:325
Sparse Core Ops, SparseCore 0:
  162.0 88.6 reduce-scatter.1

commit v2 on v1

--- a/solution.py
+++ b/solution.py
@@ -11,6 +11,7 @@
 PLANE = 4
 PIECES = 2
 VMEM_LIMIT = 56 * 1024 * 1024
+SHARE_TILE = 256
 
 
 def pack_kernel(n, capp, ids_ref, probs_ref, saved_ref, send_ref, meta_ref):
@@ -176,6 +177,263 @@
         c.wait()
 
 
+def gather_kernel(
+    dp, n, own, xs, meta, g, x, m, local_sem, a_send, up_sem, down_sem, y_sem, core_sem,
+    x_send, x_recv, m_send, m_recv, g_recv, fx_send, fm_send
+):
+    me = lax.axis_index("expert")
+    r = lax.axis_index("dp")
+    depth = n // PLANE
+    z = me // PLANE
+    lane = lax.rem(me, PLANE)
+    core_lane = lane + 1 - 2 * lax.rem(lane, 2)
+    y_lane = lax.rem(lane + 2, PLANE)
+    core_mate = z * PLANE + core_lane
+    y_mate = z * PLANE + y_lane
+    reps = [lax.rem(r + k, dp) for k in range(dp)]
+
+    barrier = pltpu.get_barrier_semaphore()
+    for d in range(1, n):
+        pl.semaphore_signal(barrier, inc=1, device_id={"expert": lax.rem(me + d, n)})
+    for k in range(1, dp):
+        pl.semaphore_signal(barrier, inc=1, device_id={"dp": reps[k]})
+    pl.semaphore_wait(barrier, n - 1 + dp - 1)
+
+    def across(k):
+        return pltpu.make_async_remote_copy(
+            src_ref=own.at[reps[k]], dst_ref=g.at[r, me], send_sem=a_send.at[k], recv_sem=g_recv.at[r, me],
+            device_id={"dp": reps[k]},
+        )
+
+    def cp(block, k, dest, send, from_own=False):
+        return pltpu.make_async_remote_copy(
+            src_ref=own.at[r] if from_own else g.at[reps[k], block],
+            dst_ref=g.at[reps[k], block],
+            send_sem=send,
+            recv_sem=g_recv.at[reps[k], block],
+            device_id={"expert": dest},
+        )
+
+    def got(block, k):
+        cp(block, k, me, up_sem.at[0, k]).wait_recv()
+
+    def hand_on(bz, k, up, down, from_own=False):
+        block = bz * PLANE + lane
+        if up:
+            @pl.when(z + 1 < depth)
+            def _():
+                cp(block, k, me + PLANE, up_sem.at[bz, k], from_own).start()
+        if down:
+            @pl.when(z >= 1)
+            def _():
+                cp(block, k, me - PLANE, down_sem.at[bz, k], from_own).start()
+        cp(block, k, y_mate, y_sem.at[bz, k], from_own).start()
+        cp(block, k, core_mate, core_sem.at[bz, k], from_own).start()
+
+    for k in range(1, dp):
+        across(k).start()
+    hand_on(z, 0, True, True, from_own=True)
+
+    locals_ = [
+        pltpu.make_async_copy(own.at[r], g.at[r, me], local_sem.at[0]),
+        pltpu.make_async_copy(xs.at[me], x.at[r, me], local_sem.at[1]),
+        pltpu.make_async_copy(meta, m.at[r, me], local_sem.at[2]),
+    ]
+    for c in locals_:
+        c.start()
+
+    def xcp(d):
+        dest = lax.rem(me + d, n)
+        return pltpu.make_async_remote_copy(
+            src_ref=xs.at[dest], dst_ref=x.at[r, me], send_sem=x_send.at[d], recv_sem=x_recv.at[r, me],
+            device_id={"expert": dest},
+        )
+
+    def mcp(d):
+        return pltpu.make_async_remote_copy(
+            src_ref=meta, dst_ref=m.at[r, me], send_sem=m_send.at[d], recv_sem=m_recv.at[r, me],
+            device_id={"expert": lax.rem(me + d, n)},
+        )
+
+    for d in range(1, n):
+        mcp(d).start()
+        xcp(d).start()
+
+    def forward(s, k, own_block=False):
+        return (
+            pltpu.make_async_remote_copy(
+                src_ref=xs.at[s] if own_block else x.at[r, s], dst_ref=x.at[r, s],
+                send_sem=fx_send.at[k, s], recv_sem=x_recv.at[r, s], device_id={"dp": reps[k]},
+            ),
+            pltpu.make_async_remote_copy(
+                src_ref=meta if own_block else m.at[r, s], dst_ref=m.at[r, s],
+                send_sem=fm_send.at[k, s], recv_sem=m_recv.at[r, s], device_id={"dp": reps[k]},
+            ),
+        )
+
+    def arrived(rep, s):
+        pltpu.make_async_remote_copy(
+            src_ref=x.at[rep, s], dst_ref=x.at[rep, s], send_sem=x_send.at[0], recv_sem=x_recv.at[rep, s],
+            device_id={"dp": r},
+        ).wait_recv()
+        pltpu.make_async_remote_copy(
+            src_ref=m.at[rep, s], dst_ref=m.at[rep, s], send_sem=m_send.at[0], recv_sem=m_recv.at[rep, s],
+            device_id={"dp": r},
+        ).wait_recv()
+
+    def slots_of_plane(pz):
+        for i in range(PLANE):
+            arrived(r, pz * PLANE + i)
+            for k in range(1, dp):
+                for c in forward(pz * PLANE + i, k):
+                    c.start()
+
+    for k in range(1, dp):
+        for c in forward(me, k, True):
+            c.start()
+        got(me, k)
+        hand_on(z, k, True, True)
+
+    def relay(bz, k):
+        block = bz * PLANE + y_lane
+        got(block, k)
+        cp(block, k, core_mate, core_sem.at[depth + bz, k]).start()
+
+    for step in range(1, depth + 1):
+        last = step - 1
+        for k in range(dp):
+            if step < depth:
+                @pl.when(z - step >= 0)
+                def _():
+                    got((z - step) * PLANE + lane, k)
+                    hand_on(z - step, k, True, False)
+
+                @pl.when(z + step < depth)
+                def _():
+                    got((z + step) * PLANE + lane, k)
+                    hand_on(z + step, k, False, True)
+            @pl.when(z - last >= 0)
+            def _():
+                relay(z - last, k)
+
+            if last:
+                @pl.when(z + last < depth)
+                def _():
+                    relay(z + last, k)
+        if last == 0:
+            for i in range(1, PLANE):
+                s = z * PLANE + lax.rem(lane + i, PLANE)
+                arrived(r, s)
+                for k in range(1, dp):
+                    for c in forward(s, k):
+                        c.start()
+        else:
+            @pl.when(z - last >= 0)
+            def _():
+                slots_of_plane(z - last)
+
+            @pl.when(z + last < depth)
+            def _():
+                slots_of_plane(z + last)
+
+    for bz in range(depth):
+        for k in range(dp):
+            got(bz * PLANE + core_lane, k)
+            got(bz * PLANE + lax.rem(core_lane + 2, PLANE), k)
+    for k in range(1, dp):
+        for s in range(n):
+            arrived(reps[k], s)
+    for d in range(1, n):
+        xcp(d).wait_send()
+        mcp(d).wait_send()
+    for k in range(1, dp):
+        across(k).wait_send()
+        for s in range(n):
+            for c in forward(s, k):
+                c.wait_send()
+    for bz in range(depth):
+        for k in range(dp):
+            block = bz * PLANE + lane
+
+            @pl.when((z + 1 < depth) & (bz <= z))
+            def _():
+                cp(block, k, me, up_sem.at[bz, k]).wait_send()
+
+            @pl.when((z >= 1) & (bz >= z))
+            def _():
+                cp(block, k, me, down_sem.at[bz, k]).wait_send()
+
+            cp(block, k, y_mate, y_sem.at[bz, k]).wait_send()
+            cp(block, k, core_mate, core_sem.at[bz, k]).wait_send()
+            cp(block, k, core_mate, core_sem.at[depth + bz, k]).wait_send()
+    for c in locals_:
+        c.wait()
+
+
+def return_kernel(dp, n, part, ret, inbox, total, a_send, a_recv, local_sem, send, recv):
+    me = lax.axis_index("expert")
+    r = lax.axis_index("dp")
+    depth = n // PLANE
+    z = me // PLANE
+    lane = lax.rem(me, PLANE)
+    reps = [lax.rem(r + k, dp) for k in range(dp)]
+    planes = [lax.rem(z + 1 + i, depth) * PLANE for i in range(depth)]
+
+    barrier = pltpu.get_barrier_semaphore()
+    for d in range(1, n):
+        pl.semaphore_signal(barrier, inc=1, device_id={"expert": lax.rem(me + d, n)})
+    for k in range(1, dp):
+        pl.semaphore_signal(barrier, inc=1, device_id={"dp": reps[k]})
+    pl.semaphore_wait(barrier, n - 1 + dp - 1)
+
+    def across(i, k):
+        return pltpu.make_async_remote_copy(
+            src_ref=part.at[reps[k], pl.ds(planes[i], PLANE)],
+            dst_ref=inbox.at[dp - k - 1, pl.ds(planes[i], PLANE)],
+            send_sem=a_send.at[k - 1, i],
+            recv_sem=a_recv.at[dp - k - 1, i],
+            device_id={"dp": reps[k]},
+        )
+
+    def back(dest):
+        return pltpu.make_async_remote_copy(
+            src_ref=total.at[dest], dst_ref=ret.at[me], send_sem=send.at[dest], recv_sem=recv.at[me],
+            device_id={"expert": dest},
+        )
+
+    for i in range(depth):
+        for k in range(1, dp):
+            across(i, k).start()
+    for i in range(depth):
+        for k in range(1, dp):
+            across(i, k).wait_recv()
+        for j in range(PLANE):
+            row = planes[i] + j
+            value = part[r, row].astype(jnp.float32)
+            for k in range(1, dp):
+                value = value + inbox[k - 1, row].astype(jnp.float32)
+            total[row] = value.astype(jnp.bfloat16)
+        for j in range(PLANE):
+            if i < depth - 1:
+                back(planes[i] + j).start()
+            elif j:
+                back(z * PLANE + lax.rem(lane + j, PLANE)).start()
+    mine = pltpu.make_async_copy(total.at[me], ret.at[me], local_sem.at[0])
+    mine.start()
+    for d in range(1, n):
+        peer = lax.rem(me + d, n)
+        pltpu.make_async_remote_copy(
+            src_ref=total.at[peer], dst_ref=ret.at[peer], send_sem=send.at[peer], recv_sem=recv.at[peer],
+            device_id={"expert": peer},
+        ).wait_recv()
+    for d in range(1, n):
+        back(lax.rem(me + d, n)).wait_send()
+    for i in range(depth):
+        for k in range(1, dp):
+            across(i, k).wait_send()
+    mine.wait()
+
+
 def powers_of(exponents):
     one = jnp.ones_like(exponents)
     up = jnp.left_shift(one, -exponents).astype(jnp.float32)
@@ -231,6 +489,174 @@
         codes = w_ref[:, cols].astype(jnp.float32) * up[:, j : j + 1]
         inside = ((codes >= -8.5) & (codes <= 7.5)).astype(jnp.float32)
         o_ref[:, cols] = s_ref[:, cols].astype(jnp.float32) * inside
+
+
+def pick_slots(sources, capp, top, me, m_ref, sel, prob):
+    slots, tok = m_ref.shape[2], sel.shape[2]
+    places = lax.broadcasted_iota(jnp.int32, (capp, slots), 0) + me * capp
+    slot = lax.broadcasted_iota(jnp.int32, (slots, tok), 0)
+    first = lax.broadcasted_iota(jnp.int32, (slots, tok), 1) * top
+    owner = ((slot >= first) & (slot < first + top)).astype(jnp.float32).astype(jnp.bfloat16)
+
+    @pl.loop(0, sources)
+    def _(s):
+        here = (places == m_ref[s, 0:1, :].astype(jnp.int32)).astype(jnp.float32)
+        sel[s] = jnp.dot(
+            here.astype(jnp.bfloat16), owner, preferred_element_type=jnp.float32
+        ).astype(jnp.bfloat16)
+        weight = jnp.sum(here * m_ref[s, 1:2, :], axis=1, keepdims=True)
+        prob[s] = jnp.broadcast_to(weight, prob.shape[1:])
+
+
+def share_kernel(sources, capp, top, at_ref, m_ref, g_ref, x_ref, w_ref, e_ref, back_ref, o_ref, sel, prob, sg, wq, acc):
+    step = pl.program_id(0)
+    tok = g_ref.shape[0] // sources
+
+    @pl.when(step == 0)
+    def _():
+        acc[...] = jnp.zeros_like(acc)
+        pick_slots(sources, capp, top, at_ref[1], m_ref, sel, prob)
+
+    for s in range(sources):
+        picked = jnp.dot(sel[s], g_ref[s * tok : (s + 1) * tok, :], preferred_element_type=jnp.float32)
+        sg[s * capp : (s + 1) * capp, :] = (picked * prob[s][:, 0:1]).astype(jnp.bfloat16)
+    grads = lax.dot_general(
+        sg[...], x_ref[...], (((0,), (0,)), ((), ())), preferred_element_type=jnp.float32
+    )
+    up, down = powers_of(e_ref[...])
+    for j in range(e_ref.shape[1]):
+        cols = slice(j * BLK, (j + 1) * BLK)
+        codes = w_ref[:, cols].astype(jnp.float32) * up[:, j : j + 1]
+        levels = jnp.clip(jnp.floor(codes + 0.5), -8.0, 7.0)
+        wq[:, cols] = (levels * down[:, j : j + 1]).astype(jnp.bfloat16)
+        inside = ((codes >= -8.5) & (codes <= 7.5)).astype(jnp.float32)
+        o_ref[:, cols] = grads[:, cols] * inside
+    acc[...] += jnp.dot(sg[...], wq[...], preferred_element_type=jnp.float32)
+
+    @pl.when(step == pl.num_programs(0) - 1)
+    def _():
+        back_ref[...] = acc[...].astype(jnp.bfloat16)
+
+
+def pack(n, capp, route_probs, expert_ids, saved_inputs):
+    tok, top = expert_ids.shape
+    slots, hidden = tok * top, saved_inputs.shape[2]
+    vmem = pl.BlockSpec(memory_space=pltpu.VMEM)
+    return pl.pallas_call(
+        functools.partial(pack_kernel, n, capp),
+        out_shape=(
+            jax.ShapeDtypeStruct((n, capp, hidden), jnp.bfloat16),
+            jax.ShapeDtypeStruct((8, slots), jnp.float32),
+        ),
+        in_specs=[vmem] * 3,
+        out_specs=(vmem, vmem),
+        compiler_params=pltpu.CompilerParams(vmem_limit_bytes=VMEM_LIMIT),
+        name="pack_slots",
+    )(expert_ids.reshape(1, slots), route_probs.reshape(1, slots), saved_inputs.reshape(slots, hidden))
+
+
+def local_shares(out_grads, route_probs, expert_ids, saved_inputs, w_latent, block_exponents):
+    dp, n = lax.axis_size("dp"), lax.axis_size("expert")
+    tok, top = expert_ids.shape
+    width = out_grads.shape[1]
+    hidden = saved_inputs.shape[2]
+    slots = tok * top
+    capp = -(-(tok * top * 3 // (2 * n)) // 16) * 16
+    blocks = block_exponents.shape[2]
+    bf16, f32 = jnp.bfloat16, jnp.float32
+    share, depth, sources = width // dp, n // PLANE, dp * n
+    vmem = pl.BlockSpec(memory_space=pltpu.VMEM)
+    anyspace = pl.BlockSpec(memory_space=pl.ANY)
+    dma = pltpu.SemaphoreType.DMA
+
+    own = out_grads.reshape(tok, dp, share).transpose(1, 0, 2)
+    sends, meta = pack(n, capp, route_probs, expert_ids, saved_inputs)
+    g, x, m = pl.pallas_call(
+        functools.partial(gather_kernel, dp, n),
+        out_shape=(
+            jax.ShapeDtypeStruct((dp, n, tok, share), bf16),
+            jax.ShapeDtypeStruct((dp, n, capp, hidden), bf16),
+            jax.ShapeDtypeStruct((dp, n, 8, slots), f32),
+        ),
+        in_specs=[anyspace] * 3,
+        out_specs=(anyspace,) * 3,
+        scratch_shapes=[
+            dma((3,)),
+            dma((dp,)),
+            dma((depth, dp)),
+            dma((depth, dp)),
+            dma((depth, dp)),
+            dma((2 * depth, dp)),
+            dma((n,)),
+            dma((dp, n)),
+            dma((n,)),
+            dma((dp, n)),
+            dma((dp, n)),
+            dma((dp, n)),
+            dma((dp, n)),
+        ],
+        compiler_params=pltpu.CompilerParams(collective_id=0, has_side_effects=True),
+        name="gather",
+    )(own, sends, meta)
+
+    tile = SHARE_TILE
+    tiles = share // tile
+    at = jnp.stack([lax.axis_index("dp") * tiles, lax.axis_index("expert")]).astype(jnp.int32)
+    back, weight_grads = pl.pallas_call(
+        functools.partial(share_kernel, sources, capp, top),
+        grid_spec=pltpu.PrefetchScalarGridSpec(
+            num_scalar_prefetch=1,
+            grid=(tiles,),
+            in_specs=[
+                pl.BlockSpec((sources, 8, slots), lambda i, at: (0, 0, 0)),
+                pl.BlockSpec((sources * tok, tile), lambda i, at: (0, i)),
+                pl.BlockSpec((sources * capp, hidden), lambda i, at: (0, 0)),
+                pl.BlockSpec((tile, hidden), lambda i, at: (at[0] + i, 0)),
+                pl.BlockSpec((tile, blocks), lambda i, at: (at[0] + i, 0)),
+            ],
+            out_specs=(
+                pl.BlockSpec((sources * capp, hidden), lambda i, at: (0, 0)),
+                pl.BlockSpec((tile, hidden), lambda i, at: (i, 0)),
+            ),
+            scratch_shapes=[
+                pltpu.VMEM((sources, capp, tok), bf16),
+                pltpu.VMEM((sources, capp, 128), f32),
+                pltpu.VMEM((sources * capp, tile), bf16),
+                pltpu.VMEM((tile, hidden), bf16),
+                pltpu.VMEM((sources * capp, hidden), f32),
+            ],
+        ),
+        out_shape=(
+            jax.ShapeDtypeStruct((sources * capp, hidden), bf16),
+            jax.ShapeDtypeStruct((share, hidden), f32),
+        ),
+        compiler_params=pltpu.CompilerParams(vmem_limit_bytes=VMEM_LIMIT),
+        name="share",
+    )(at, m.reshape(sources, 8, slots), g.reshape(sources * tok, share), x.reshape(sources * capp, hidden),
+      w_latent[0], block_exponents[0])
+
+    returned = pl.pallas_call(
+        functools.partial(return_kernel, dp, n),
+        out_shape=jax.ShapeDtypeStruct((n, capp, hidden), bf16),
+        in_specs=[vmem],
+        out_specs=anyspace,
+        scratch_shapes=[
+            pltpu.VMEM((dp - 1, n, capp, hidden), bf16),
+            pltpu.VMEM((n, capp, hidden), bf16),
+            dma((dp - 1, depth)),
+            dma((dp - 1, depth)),
+            dma((1,)),
+            dma((n,)),
+            dma((n,)),
+        ],
+        compiler_params=pltpu.CompilerParams(
+            collective_id=1, has_side_effects=True, vmem_limit_bytes=VMEM_LIMIT
+        ),
+        name="give_back",
+    )(back.reshape(dp, n, capp, hidden))
+    target = meta[0].astype(jnp.int32)
+    input_grads = returned.reshape(n * capp, hidden)[target].reshape(tok, top, hidden)
+    return (input_grads, weight_grads[None])
 
 
 def tile_of(size, most):
@@ -361,8 +787,15 @@
         P("expert", None, None),
         P("expert", None, None),
     )
+    dp = mesh.shape["dp"]
+
+    def body(out_grads, *rest):
+        share = out_grads.shape[1] // dp
+        plan = local_shares if dp == 2 and share % SHARE_TILE == 0 else local
+        return plan(out_grads, *rest)
+
     return jax.shard_map(
-        local,
+        body,
         mesh=mesh,
         in_specs=placed,
         out_specs=(P(("dp", "expert"), None, None), P("expert", "dp", None)),

time: 268 us -> 224 us (0.84)
  waiting for transfers between devices: 79.9 us -> 0 us
  Pallas kernels: 157 us -> 208 us
  between operations: 14.1 us -> 0.69 us
  starting transfers between devices: 4.88 us -> 0 us
  local copies, waits for them, and re-layouts: 10.1 us -> 14.3 us
    pallas_call x4, Pallas kernels: 157 us -> 208 us  [the longest x1 122 us: local_shares(): pl.pallas_call(functools.partial(gather_kernel, dp, n), out_shape=(jax.Sh...]
    reduce_scatter x1 -> x0, waiting for transfers between devices: 48.7 us -> none  [local(): summed = lax.psum_scatter(partial, 'dp', scatter_dimension=0, tiled=True)]
    all_to_all x1 -> x0, waiting for transfers between devices: 31.2 us -> none  [local(): lax.all_to_all(back.reshape(n, capp, hidden), 'expert', split_axis=0, con...]
    all_to_all x1 -> x0, starting transfers between devices: 4.85 us -> none  [local(): lax.all_to_all(back.reshape(n, capp, hidden), 'expert', split_axis=0, con...]
  transfers between devices with their start and end apart: 2 -> 0, of which waited for: 2 -> 0; matrix products, arithmetic and copies ran while one was open for 1% -> 0% of each run, Pallas kernels for 0% -> 0%
where the time goes in v2:
time: 224 us
  Pallas kernels  208 us (93%)
  local copies, waits for them, and re-layouts  14.3 us (6%)
    pallas_call x1, Pallas kernels, local_shares(): pl.pallas_call(functools.partial(gather_kernel, dp, n), out_shape=(jax.Sh...  122 us
    pallas_call x1, Pallas kernels, local_shares(): pl.pallas_call(functools.partial(return_kernel, dp, n), out_shape=jax.Sha...  50.4 us
    pallas_call x1, Pallas kernels, local_shares(): pl.pallas_call(functools.partial(share_kernel, sources, capp, top), grid_...  28.2 us
    pallas_call x1, Pallas kernels, pack(): pl.pallas_call(functools.partial(pack_kernel, n, capp), out_shape=(jax.Sh...  7.31 us
    unnamed x8, local copies, waits for them, and re-layouts  4.99 us

profile of v2, /device:TPU:0, one launch (start us, length us, event | category | flops | bytes accessed | tf_op | source)
XLA Modules:
  0.0 223.9 jit_solution(3090742189811981749)
XLA Ops:
  0.6 0.0 copy-start
  0.6 0.6 pad_add_fusion.at_ref
  1.2 0.8 copy.14
  2.0 0.7 reshape.56.probs_ref
  2.7 0.8 copy.13
  3.5 0.7 reshape.55.ids_ref
  4.2 0.0 copy-start.1
  4.2 1.6 copy.11
  5.8 1.3 copy.12
  7.1 0.0 copy-done
  7.1 1.1 reshape.57.saved_ref
  8.2 7.3 %pack_slots.1 = (bf16[16,48,1024]{2,1,0:T(8,128)(2,1)}, f32[8,512]{1,0:T(8,128)}) custom-call(s32[1,512]{1,0:T(1,128)} %reshape.55.ids_ref, f32[1,512]{1,0:T(1,128)} %reshape.56.probs_ref, bf16[512,1024]{1,0:T(8,128)(2,1)} %reshape.57.saved_ref), custom_call_target="tpu_custom_call" | custom-call | tf_op jit(solution)/shard_map/pack_slots/pallas_call | solution.py:545
  15.5 0.7 compare_select_fusion
  16.2 0.0 copy-done.1
  16.2 1.8 copy.15
  18.1 121.6 %gather.7 = (bf16[2,16,128,1792]{3,2,1,0:T(8,128)(2,1)}, bf16[2,16,48,1024]{3,2,1,0:T(8,128)(2,1)}, f32[2,16,8,512]{3,2,1,0:T(8,128)}) custom-call(bf16[2,128,1792]{2,1,0:T(8,128)(2,1)} %bitcast.20, bf16[16,48,1024]{2,1,0:T(8,128)(2,1)} %get-tuple-element.9.xs, f32[8,512]{1,0:T(8,128)} %get-tuple-element.10.meta), custom_call_target="tpu_custom_call" | custom-call | tf_op jit(solution)/shard_map/gather/pallas_call | solution.py:574
  139.7 28.2 %share.1 = (bf16[1536,1024]{1,0:T(8,128)(2,1)}, f32[1792,1024]{1,0:T(8,128)}) custom-call(s32[2]{0:T(128)} %pad_add_fusion.at_ref, f32[32,8,512]{2,1,0:T(8,128)} %bitcast.23, bf16[4096,1792]{1,0:T(8,128)(2,1)} %bitcast.16, bf16[1536,1024]{1,0:T(8,128)(2,1)} %bitcast.21, bf16[3584,1024]{1,0:T(8,128)(2,1)} %bitcast.18, s32[3584,8]{1,0:T(8,128)} %bitcast.17), custom_call_target="tpu_custom_call" | custom-call | tf_op jit(solution)/shard_map/share/pallas_call | solution.py:605
  167.9 50.4 %give_back.1 = bf16[16,48,1024]{2,1,0:T(8,128)(2,1)} custom-call(bf16[2,16,48,1024]{3,2,1,0:T(8,128)(2,1)} %bitcast.22), custom_call_target="tpu_custom_call" | custom-call | tf_op jit(solution)/shard_map/give_back/pallas_call | solution.py:638
  218.4 4.3 %gather_fusion = bf16[512,1024]{1,0:T(8,128)(2,1)S(1)} fusion(bf16[768,1024]{1,0:T(8,128)(2,1)} %bitcast.15, s32[1024]{0:T(1024)S(1)} %pad_clamp_fusion), kind=kCustom, calls=%fused_computation | custom fusion | bytes 2099200 | tf_op jit(solution)/shard_map/gather | solution.py:658
  222.7 1.2 reshape.63
  (1 shorter events, 0.0 us)
Async XLA Ops:
  0.6 6.5 %copy-start = (bf16[128,4,1024]{2,1,0:T(4,128)(2,1)S(1)}, bf16[128,4,1024]{2,1,0:T(4,128)(2,1)}, u32[]{:S(2)}) copy-start(bf16[128,4,1024]{2,1,0:T(4,128)(2,1)} %param.9) | copy-start | bytes 3145732
  4.2 12.0 %copy-start.1 = (s32[1,3584,8]{1,2,0:T(8,128)S(1)}, s32[1,3584,8]{1,2,0:T(8,128)}, u32[]{:S(2)}) copy-start(s32[1,3584,8]{1,2,0:T(8,128)} %param.11) | copy-start | bytes 344068

commit v3 on v2

--- a/solution.py
+++ b/solution.py
@@ -178,7 +178,7 @@
 
 
 def gather_kernel(
-    dp, n, own, xs, meta, g, x, m, local_sem, a_send, up_sem, down_sem, y_sem, core_sem,
+    dp, n, own, ids, probs, saved, g, x, m, meta, xs, local_sem, a_send, up_sem, down_sem, y_sem, core_sem,
     x_send, x_recv, m_send, m_recv, g_recv, fx_send, fm_send
 ):
     me = lax.axis_index("expert")
@@ -191,6 +191,13 @@
     core_mate = z * PLANE + core_lane
     y_mate = z * PLANE + y_lane
     reps = [lax.rem(r + k, dp) for k in range(dp)]
+    rows, share = own.shape[0] // PIECES, own.shape[1] // dp
+
+    def own_part(rep, p):
+        return own.at[pl.ds(p * rows, rows), pl.ds(pl.multiple_of(rep * share, BLK), share)]
+
+    def g_part(rep, block, p):
+        return g.at[rep, block, pl.ds(p * rows, rows)]
 
     barrier = pltpu.get_barrier_semaphore()
     for d in range(1, n):
@@ -199,43 +206,47 @@
         pl.semaphore_signal(barrier, inc=1, device_id={"dp": reps[k]})
     pl.semaphore_wait(barrier, n - 1 + dp - 1)
 
-    def across(k):
+    def across(k, p):
         return pltpu.make_async_remote_copy(
-            src_ref=own.at[reps[k]], dst_ref=g.at[r, me], send_sem=a_send.at[k], recv_sem=g_recv.at[r, me],
-            device_id={"dp": reps[k]},
-        )
-
-    def cp(block, k, dest, send, from_own=False):
+            src_ref=own_part(reps[k], p), dst_ref=g_part(r, me, p), send_sem=a_send.at[k, p],
+            recv_sem=g_recv.at[r, me, p], device_id={"dp": reps[k]},
+        )
+
+    def cp(block, k, p, dest, send, from_own=False):
         return pltpu.make_async_remote_copy(
-            src_ref=own.at[r] if from_own else g.at[reps[k], block],
-            dst_ref=g.at[reps[k], block],
+            src_ref=own_part(r, p) if from_own else g_part(reps[k], block, p),
+            dst_ref=g_part(reps[k], block, p),
             send_sem=send,
-            recv_sem=g_recv.at[reps[k], block],
+            recv_sem=g_recv.at[reps[k], block, p],
             device_id={"expert": dest},
         )
 
-    def got(block, k):
-        cp(block, k, me, up_sem.at[0, k]).wait_recv()
-
-    def hand_on(bz, k, up, down, from_own=False):
+    def got(block, k, p):
+        cp(block, k, p, me, up_sem.at[0, k, p]).wait_recv()
+
+    def hand_on(bz, k, p, up, down, from_own=False):
         block = bz * PLANE + lane
         if up:
             @pl.when(z + 1 < depth)
             def _():
-                cp(block, k, me + PLANE, up_sem.at[bz, k], from_own).start()
+                cp(block, k, p, me + PLANE, up_sem.at[bz, k, p], from_own).start()
         if down:
             @pl.when(z >= 1)
             def _():
-                cp(block, k, me - PLANE, down_sem.at[bz, k], from_own).start()
-        cp(block, k, y_mate, y_sem.at[bz, k], from_own).start()
-        cp(block, k, core_mate, core_sem.at[bz, k], from_own).start()
-
-    for k in range(1, dp):
-        across(k).start()
-    hand_on(z, 0, True, True, from_own=True)
+                cp(block, k, p, me - PLANE, down_sem.at[bz, k, p], from_own).start()
+        cp(block, k, p, y_mate, y_sem.at[bz, k, p], from_own).start()
+        cp(block, k, p, core_mate, core_sem.at[bz, k, p], from_own).start()
+
+    for p in range(PIECES):
+        for k in range(1, dp):
+            across(k, p).start()
+        hand_on(z, 0, p, True, True, from_own=True)
+    pack_kernel(n, xs.shape[1], ids, probs, saved, xs, meta)
 
     locals_ = [
-        pltpu.make_async_copy(own.at[r], g.at[r, me], local_sem.at[0]),
+        pltpu.make_async_copy(
+            own.at[:, pl.ds(pl.multiple_of(r * share, BLK), share)], g.at[r, me], local_sem.at[0]
+        ),
         pltpu.make_async_copy(xs.at[me], x.at[r, me], local_sem.at[1]),
         pltpu.make_async_copy(meta, m.at[r, me], local_sem.at[2]),
     ]
@@ -291,35 +302,37 @@
     for k in range(1, dp):
         for c in forward(me, k, True):
             c.start()
-        got(me, k)
-        hand_on(z, k, True, True)
-
-    def relay(bz, k):
+        for p in range(PIECES):
+            got(me, k, p)
+            hand_on(z, k, p, True, True)
+
+    def relay(bz, k, p):
         block = bz * PLANE + y_lane
-        got(block, k)
-        cp(block, k, core_mate, core_sem.at[depth + bz, k]).start()
-
+        got(block, k, p)
+        cp(block, k, p, core_mate, core_sem.at[depth + bz, k, p]).start()
+
+    both = [(k, p) for k in range(dp) for p in range(PIECES)]
     for step in range(1, depth + 1):
         last = step - 1
-        for k in range(dp):
+        for k, p in both:
             if step < depth:
                 @pl.when(z - step >= 0)
                 def _():
-                    got((z - step) * PLANE + lane, k)
-                    hand_on(z - step, k, True, False)
+                    got((z - step) * PLANE + lane, k, p)
+                    hand_on(z - step, k, p, True, False)
 
                 @pl.when(z + step < depth)
                 def _():
-                    got((z + step) * PLANE + lane, k)
-                    hand_on(z + step, k, False, True)
+                    got((z + step) * PLANE + lane, k, p)
+                    hand_on(z + step, k, p, False, True)
             @pl.when(z - last >= 0)
             def _():
-                relay(z - last, k)
+                relay(z - last, k, p)
 
             if last:
                 @pl.when(z + last < depth)
                 def _():
-                    relay(z + last, k)
+                    relay(z + last, k, p)
         if last == 0:
             for i in range(1, PLANE):
                 s = z * PLANE + lax.rem(lane + i, PLANE)
@@ -337,9 +350,9 @@
                 slots_of_plane(z + last)
 
     for bz in range(depth):
-        for k in range(dp):
-            got(bz * PLANE + core_lane, k)
-            got(bz * PLANE + lax.rem(core_lane + 2, PLANE), k)
+        for k, p in both:
+            got(bz * PLANE + core_lane, k, p)
+            got(bz * PLANE + lax.rem(core_lane + 2, PLANE), k, p)
     for k in range(1, dp):
         for s in range(n):
             arrived(reps[k], s)
@@ -347,25 +360,26 @@
         xcp(d).wait_send()
         mcp(d).wait_send()
     for k in range(1, dp):
-        across(k).wait_send()
+        for p in range(PIECES):
+            across(k, p).wait_send()
         for s in range(n):
             for c in forward(s, k):
                 c.wait_send()
     for bz in range(depth):
-        for k in range(dp):
+        for k, p in both:
             block = bz * PLANE + lane
 
             @pl.when((z + 1 < depth) & (bz <= z))
             def _():
-                cp(block, k, me, up_sem.at[bz, k]).wait_send()
+                cp(block, k, p, me, up_sem.at[bz, k, p]).wait_send()
 
             @pl.when((z >= 1) & (bz >= z))
             def _():
-                cp(block, k, me, down_sem.at[bz, k]).wait_send()
-
-            cp(block, k, y_mate, y_sem.at[bz, k]).wait_send()
-            cp(block, k, core_mate, core_sem.at[bz, k]).wait_send()
-            cp(block, k, core_mate, core_sem.at[depth + bz, k]).wait_send()
+                cp(block, k, p, me, down_sem.at[bz, k, p]).wait_send()
+
+            cp(block, k, p, y_mate, y_sem.at[bz, k, p]).wait_send()
+            cp(block, k, p, core_mate, core_sem.at[bz, k, p]).wait_send()
+            cp(block, k, p, core_mate, core_sem.at[depth + bz, k, p]).wait_send()
     for c in locals_:
         c.wait()
 
@@ -377,7 +391,10 @@
     z = me // PLANE
     lane = lax.rem(me, PLANE)
     reps = [lax.rem(r + k, dp) for k in range(dp)]
-    planes = [lax.rem(z + 1 + i, depth) * PLANE for i in range(depth)]
+    order = sorted(range(1, depth), key=lambda o: abs(2 * o - depth)) + [0]
+    half = PLANE // 2
+    groups = [lax.rem(z + o, depth) * PLANE + h for o in order for h in (0, half)]
+    count = len(groups)
 
     barrier = pltpu.get_barrier_semaphore()
     for d in range(1, n):
@@ -388,8 +405,8 @@
 
     def across(i, k):
         return pltpu.make_async_remote_copy(
-            src_ref=part.at[reps[k], pl.ds(planes[i], PLANE)],
-            dst_ref=inbox.at[dp - k - 1, pl.ds(planes[i], PLANE)],
+            src_ref=part.at[reps[k], pl.ds(groups[i], half)],
+            dst_ref=inbox.at[dp - k - 1, pl.ds(groups[i], half)],
             send_sem=a_send.at[k - 1, i],
             recv_sem=a_recv.at[dp - k - 1, i],
             device_id={"dp": reps[k]},
@@ -401,23 +418,23 @@
             device_id={"expert": dest},
         )
 
-    for i in range(depth):
+    for i in range(count):
         for k in range(1, dp):
             across(i, k).start()
-    for i in range(depth):
+    for i in range(count):
         for k in range(1, dp):
             across(i, k).wait_recv()
-        for j in range(PLANE):
-            row = planes[i] + j
+        for j in range(half):
+            row = groups[i] + j
             value = part[r, row].astype(jnp.float32)
             for k in range(1, dp):
                 value = value + inbox[k - 1, row].astype(jnp.float32)
             total[row] = value.astype(jnp.bfloat16)
-        for j in range(PLANE):
-            if i < depth - 1:
-                back(planes[i] + j).start()
-            elif j:
-                back(z * PLANE + lax.rem(lane + j, PLANE)).start()
+        if i < count - 2:
+            for j in range(half):
+                back(groups[i] + j).start()
+    for j in range(1, PLANE):
+        back(z * PLANE + lax.rem(lane + j, PLANE)).start()
     mine = pltpu.make_async_copy(total.at[me], ret.at[me], local_sem.at[0])
     mine.start()
     for d in range(1, n):
@@ -428,7 +445,7 @@
         ).wait_recv()
     for d in range(1, n):
         back(lax.rem(me + d, n)).wait_send()
-    for i in range(depth):
+    for i in range(count):
         for k in range(1, dp):
             across(i, k).wait_send()
     mine.wait()
@@ -491,21 +508,24 @@
         o_ref[:, cols] = s_ref[:, cols].astype(jnp.float32) * inside
 
 
-def pick_slots(sources, capp, top, me, m_ref, sel, prob):
-    slots, tok = m_ref.shape[2], sel.shape[2]
+def pick_slots(sources, capp, tok, top, me, m_ref, sel, prob):
+    slots = m_ref.shape[2]
     places = lax.broadcasted_iota(jnp.int32, (capp, slots), 0) + me * capp
     slot = lax.broadcasted_iota(jnp.int32, (slots, tok), 0)
     first = lax.broadcasted_iota(jnp.int32, (slots, tok), 1) * top
     owner = ((slot >= first) & (slot < first + top)).astype(jnp.float32).astype(jnp.bfloat16)
 
-    @pl.loop(0, sources)
-    def _(s):
-        here = (places == m_ref[s, 0:1, :].astype(jnp.int32)).astype(jnp.float32)
-        sel[s] = jnp.dot(
-            here.astype(jnp.bfloat16), owner, preferred_element_type=jnp.float32
-        ).astype(jnp.bfloat16)
-        weight = jnp.sum(here * m_ref[s, 1:2, :], axis=1, keepdims=True)
-        prob[s] = jnp.broadcast_to(weight, prob.shape[1:])
+    @pl.loop(0, sources // 2)
+    def _(pair):
+        sel[pair] = jnp.zeros(sel.shape[1:], sel.dtype)
+        for h in range(2):
+            at = slice(h * capp, (h + 1) * capp)
+            here = (places == m_ref[2 * pair + h, 0:1, :].astype(jnp.int32)).astype(jnp.float32)
+            sel[pair, at, h * tok : (h + 1) * tok] = jnp.dot(
+                here.astype(jnp.bfloat16), owner, preferred_element_type=jnp.float32
+            ).astype(jnp.bfloat16)
+            weight = jnp.sum(here * m_ref[2 * pair + h, 1:2, :], axis=1, keepdims=True)
+            prob[pair, at, :] = jnp.broadcast_to(weight, (capp, prob.shape[2]))
 
 
 def share_kernel(sources, capp, top, at_ref, m_ref, g_ref, x_ref, w_ref, e_ref, back_ref, o_ref, sel, prob, sg, wq, acc):
@@ -515,11 +535,13 @@
     @pl.when(step == 0)
     def _():
         acc[...] = jnp.zeros_like(acc)
-        pick_slots(sources, capp, top, at_ref[1], m_ref, sel, prob)
-
-    for s in range(sources):
-        picked = jnp.dot(sel[s], g_ref[s * tok : (s + 1) * tok, :], preferred_element_type=jnp.float32)
-        sg[s * capp : (s + 1) * capp, :] = (picked * prob[s][:, 0:1]).astype(jnp.bfloat16)
+        pick_slots(sources, capp, tok, top, at_ref[1], m_ref, sel, prob)
+
+    for s in range(sources // 2):
+        pair = slice(2 * s * tok, 2 * (s + 1) * tok)
+        picked = jnp.dot(sel[s], g_ref[pair, :], preferred_element_type=jnp.float32)
+        weight = jnp.concatenate([prob[s]] * (picked.shape[1] // prob.shape[2]), axis=1)
+        sg[2 * s * capp : 2 * (s + 1) * capp, :] = (picked * weight).astype(jnp.bfloat16)
     grads = lax.dot_general(
         sg[...], x_ref[...], (((0,), (0,)), ((), ())), preferred_element_type=jnp.float32
     )
@@ -569,35 +591,37 @@
     anyspace = pl.BlockSpec(memory_space=pl.ANY)
     dma = pltpu.SemaphoreType.DMA
 
-    own = out_grads.reshape(tok, dp, share).transpose(1, 0, 2)
-    sends, meta = pack(n, capp, route_probs, expert_ids, saved_inputs)
-    g, x, m = pl.pallas_call(
+    g, x, m, meta = pl.pallas_call(
         functools.partial(gather_kernel, dp, n),
         out_shape=(
             jax.ShapeDtypeStruct((dp, n, tok, share), bf16),
             jax.ShapeDtypeStruct((dp, n, capp, hidden), bf16),
             jax.ShapeDtypeStruct((dp, n, 8, slots), f32),
-        ),
-        in_specs=[anyspace] * 3,
-        out_specs=(anyspace,) * 3,
+            jax.ShapeDtypeStruct((8, slots), f32),
+        ),
+        in_specs=[anyspace] + [vmem] * 3,
+        out_specs=(anyspace,) * 3 + (vmem,),
         scratch_shapes=[
+            pltpu.VMEM((n, capp, hidden), bf16),
             dma((3,)),
-            dma((dp,)),
-            dma((depth, dp)),
-            dma((depth, dp)),
-            dma((depth, dp)),
-            dma((2 * depth, dp)),
+            dma((dp, PIECES)),
+            dma((depth, dp, PIECES)),
+            dma((depth, dp, PIECES)),
+            dma((depth, dp, PIECES)),
+            dma((2 * depth, dp, PIECES)),
             dma((n,)),
             dma((dp, n)),
             dma((n,)),
             dma((dp, n)),
-            dma((dp, n)),
+            dma((dp, n, PIECES)),
             dma((dp, n)),
             dma((dp, n)),
         ],
-        compiler_params=pltpu.CompilerParams(collective_id=0, has_side_effects=True),
+        compiler_params=pltpu.CompilerParams(
+            collective_id=0, has_side_effects=True, vmem_limit_bytes=VMEM_LIMIT
+        ),
         name="gather",
-    )(own, sends, meta)
+    )(out_grads, expert_ids.reshape(1, slots), route_probs.reshape(1, slots), saved_inputs.reshape(slots, hidden))
 
     tile = SHARE_TILE
     tiles = share // tile
@@ -619,8 +643,8 @@
                 pl.BlockSpec((tile, hidden), lambda i, at: (i, 0)),
             ),
             scratch_shapes=[
-                pltpu.VMEM((sources, capp, tok), bf16),
-                pltpu.VMEM((sources, capp, 128), f32),
+                pltpu.VMEM((sources // 2, 2 * capp, 2 * tok), bf16),
+                pltpu.VMEM((sources // 2, 2 * capp, 128), f32),
                 pltpu.VMEM((sources * capp, tile), bf16),
                 pltpu.VMEM((tile, hidden), bf16),
                 pltpu.VMEM((sources * capp, hidden), f32),
@@ -643,8 +667,8 @@
         scratch_shapes=[
             pltpu.VMEM((dp - 1, n, capp, hidden), bf16),
             pltpu.VMEM((n, capp, hidden), bf16),
-            dma((dp - 1, depth)),
-            dma((dp - 1, depth)),
+            dma((dp - 1, 2 * depth)),
+            dma((dp - 1, 2 * depth)),
             dma((1,)),
             dma((n,)),
             dma((n,)),

time: 224 us -> 212 us (0.946)
  Pallas kernels: 208 us -> 197 us
    pallas_call x1 -> x0, Pallas kernels: 7.31 us -> none  [pack(): pl.pallas_call(functools.partial(pack_kernel, n, capp), out_shape=(jax.Sh...]
    pallas_call x1, Pallas kernels: 28.2 us -> 25.5 us  [local_shares(): pl.pallas_call(functools.partial(share_kernel, sources, capp, top), grid_...]
    pallas_call x1, Pallas kernels: 50.4 us -> 47.8 us  [local_shares(): pl.pallas_call(functools.partial(return_kernel, dp, n), out_shape=jax.Sha...]
    unnamed x8 -> x3, local copies, waits for them, and re-layouts: 4.99 us -> 4.29 us
where the time goes in v3:
time: 212 us
  Pallas kernels  197 us (93%)
  local copies, waits for them, and re-layouts  13.3 us (6%)
    pallas_call x1, Pallas kernels, local_shares(): pl.pallas_call(functools.partial(gather_kernel, dp, n), out_shape=(jax.Sh...  123 us
    pallas_call x1, Pallas kernels, local_shares(): pl.pallas_call(functools.partial(return_kernel, dp, n), out_shape=jax.Sha...  47.8 us
    pallas_call x1, Pallas kernels, local_shares(): pl.pallas_call(functools.partial(share_kernel, sources, capp, top), grid_...  25.5 us
    gather x1, local copies, waits for them, and re-layouts, local_shares(): returned.reshape(n * capp, hidden)[target].reshape(tok, top, hidden)  4.34 us
    unnamed x3, local copies, waits for them, and re-layouts  4.29 us

profile of v3, /device:TPU:0, one launch (start us, length us, event | category | flops | bytes accessed | tf_op | source)
XLA Modules:
  0.0 211.9 jit_solution(855605862904444263)
XLA Ops:
  0.6 0.6 pad_add_fusion.at_ref
  1.2 0.8 copy.12
  2.0 0.7 reshape.52.probs
  2.7 0.8 copy.11
  3.5 0.7 reshape.51.ids
  4.2 2.1 %reshape.53.saved = bf16[512,1024]{1,0:T(8,128)(2,1)} reshape(bf16[128,4,1024]{2,1,0:T(4,128)(2,1)} %param.9) | data formatting | bytes 2097152 | tf_op jit(solution)/shard_map/reshape | solution.py:624
  6.3 2.7 %copy.13 = s32[1,3584,8]{2,1,0:T(8,128)} copy(s32[1,3584,8]{1,2,0:T(8,128)} %param.11) | data formatting | bytes 229376 | tf_op args[5]
  9.0 123.2 %gather.7 = (bf16[2,16,128,1792]{3,2,1,0:T(8,128)(2,1)}, bf16[2,16,48,1024]{3,2,1,0:T(8,128)(2,1)}, f32[2,16,8,512]{3,2,1,0:T(8,128)}, f32[8,512]{1,0:T(8,128)}) custom-call(bf16[128,3584]{1,0:T(8,128)(2,1)} %own.1, s32[1,512]{1,0:T(1,128)} %reshape.51.ids, f32[1,512]{1,0:T(1,128)} %reshape.52.probs, bf16[512,1024]{1,0:T(8,128)(2,1)} %reshape.53.saved), custom_call_target="tpu_custom_call" | custom-call | tf_op jit(solution)/shard_map/gather/pallas_call | solution.py:594
  132.2 25.5 %share.1 = (bf16[1536,1024]{1,0:T(8,128)(2,1)}, f32[1792,1024]{1,0:T(8,128)}) custom-call(s32[2]{0:T(128)} %pad_add_fusion.at_ref, f32[32,8,512]{2,1,0:T(8,128)} %bitcast.19, bf16[4096,1792]{1,0:T(8,128)(2,1)} %bitcast.14, bf16[1536,1024]{1,0:T(8,128)(2,1)} %bitcast.17, bf16[3584,1024]{1,0:T(8,128)(2,1)} %bitcast.16, s32[3584,8]{1,0:T(8,128)} %bitcast.15), custom_call_target="tpu_custom_call" | custom-call | tf_op jit(solution)/shard_map/share/pallas_call | solution.py:629
  157.7 47.8 %give_back.1 = bf16[16,48,1024]{2,1,0:T(8,128)(2,1)} custom-call(bf16[2,16,48,1024]{3,2,1,0:T(8,128)(2,1)} %bitcast.18), custom_call_target="tpu_custom_call" | custom-call | tf_op jit(solution)/shard_map/give_back/pallas_call | solution.py:662
  205.6 0.7 compare_select_fusion
  206.3 4.3 %gather_fusion = bf16[512,1024]{1,0:T(8,128)(2,1)S(1)} fusion(bf16[768,1024]{1,0:T(8,128)(2,1)} %bitcast.13, s32[1024]{0:T(1024)S(1)} %pad_clamp_fusion), kind=kCustom, calls=%fused_computation | custom fusion | bytes 2099200 | tf_op jit(solution)/shard_map/gather | solution.py:682
  210.6 1.2 reshape.59
  (1 shorter events, 0.0 us)
